TPU v7x, 32 devices: a whole 2x2x4 slice. The times are simulated.
32 devices in a mesh: row: 4 (over z), col: 8 (over y, x, core).
Axes of the slice: x: 2, y: 2, z: 4, core: 2. Of those that a mesh axis runs over, the one named last changes fastest.
Arguments:
- finetune: bfloat16 [2048, 53248], P('row', 'col'), may hold values from -6 to 6
- base_rows: bfloat16 [4096, 53248], P(('row', 'col')), may hold values from -6 to 6
- test_matrix: bfloat16 [256, 53248], P(None, 'col'), may hold values from -0.02734375 to 0.02734375
- base_lengths: int32 [32], replicated, may hold values from 0 to 128, as said below
Outputs:
- basis_out: float32 [2048, 256], P(('row', 'col'))
- coefficients: float32 [256, 53248], P('row', 'col')
Inputs may be any that keep to these rules, and one draw needn't show every extreme that they name: Number devices d = row index * 8 + col index. Devices 2m and 2m+1 hold together slab rows m * 128 to m * 128 + 127: device 2m the first base_lengths[2m] of them, device 2m+1 the rest, each from its slot 0 on, so entries 2m and 2m+1 sum to 128. In every draw some device holds 128 rows and some none. Slots past a device's count hold no slab data.
All inputs are finite; a program needn't handle non-finite values.
Results may differ from a plain program's by a relative error of at most 0.014.
Values may be sent and summed in bfloat16 or wider, within the bound.
A program may use at most 128 MiB of HBM per device.

v0:
```python
import math

import jax
import jax.numpy as jnp
from jax import lax
from jax.sharding import PartitionSpec as P


def compose(first_half, second_half, first_count):
    capacity = first_half.shape[0]
    row_ids = jnp.arange(capacity)[:, None]
    padded = jnp.concatenate([jnp.zeros_like(second_half), second_half], axis=0)
    shifted = lax.dynamic_slice_in_dim(padded, capacity - first_count, capacity, 0)
    return jnp.where(row_ids < first_count, first_half, shifted)


def orthonormal(sketched, gram_matrix):
    factor = jnp.linalg.cholesky(gram_matrix)
    identity = jnp.eye(gram_matrix.shape[0], dtype=jnp.float32)
    inverse = lax.linalg.triangular_solve(factor, identity, left_side=True, lower=True)
    return jnp.dot(sketched, inverse.T, precision=lax.Precision.HIGHEST)


def against(left_side, right_side):
    return lax.dot_general(
        left_side, right_side, (((1,), (1,)), ((), ())), preferred_element_type=jnp.float32
    )


def contract_rows(left_side, right_side):
    return lax.dot_general(
        left_side, right_side, (((0,), (0,)), ((), ())), preferred_element_type=jnp.float32
    )


def per_device(finetune, base_rows, test_matrix, base_lengths):
    col_count = lax.axis_size("col")
    row_count = lax.axis_size("row")
    col_index = lax.axis_index("col")
    row_index = lax.axis_index("row")
    capacity = base_rows.shape[0]
    half_rows = capacity // 2
    received = lax.all_to_all(base_rows, "col", split_axis=1, concat_axis=0, tiled=True)
    width_block = received.shape[1]
    grouped = received.reshape(col_count // 2, 2, capacity, width_block)
    group_lengths = lax.dynamic_slice_in_dim(
        base_lengths, row_index * col_count, col_count, 0
    ).reshape(col_count // 2, 2)[:, 0]
    composed = jax.vmap(compose)(grouped[:, 0], grouped[:, 1], group_lengths)
    base_block = composed.reshape(col_count * half_rows, width_block)
    total_rows = half_rows * col_count * row_count
    right_side = test_matrix
    basis_out = None
    coefficients = None
    for sweep_index in range(2):
        partial_value = against(finetune, right_side) - against(base_block, right_side)
        group_rows = lax.psum(partial_value, "col")
        gram_matrix = lax.psum(
            jnp.dot(group_rows.T, group_rows, precision=lax.Precision.HIGHEST), "row"
        )
        group_basis = orthonormal(group_rows, gram_matrix)
        own_basis = lax.dynamic_slice_in_dim(group_basis, col_index * half_rows, half_rows, 0)
        narrow = group_basis.astype(jnp.bfloat16)
        projected = contract_rows(narrow, finetune) - contract_rows(narrow, base_block)
        if sweep_index == 0:
            right_side = lax.psum(projected.astype(jnp.bfloat16), "row")
        else:
            basis_out = own_basis * math.sqrt(total_rows)
            coefficients = lax.psum_scatter(
                projected.astype(jnp.bfloat16), "row", scatter_dimension=0, tiled=True
            ).astype(jnp.float32)
    return (basis_out, coefficients)


def solution(mesh):
    return jax.shard_map(
        per_device,
        mesh=mesh,
        in_specs=(P("row", "col"), P(("row", "col"), None), P(None, "col"), P()),
        out_specs=(P(("row", "col"), None), P("row", "col")),
        check_vma=False,
    )
```

profile of v0, /device:TPU:0, one launch (start us, length us, event | category | flops | bytes accessed | tf_op | source)
XLA Modules:
  0.0 819.5 jit_solution(1107062623324641215)
XLA Ops:
  7.2 18.5 %copy.16 = bf16[128,53248]{0,1:T(8,128)(2,1)} copy(bf16[128,53248]{1,0:T(8,128)(2,1)} %param.8) | data formatting | bytes 27262976 | tf_op args[1]
  25.7 5.6 all-to-all-start
  31.8 5.7 fusion.37
  37.5 144.8 %all-to-all-done = bf16[128,8,6656]{0,2,1:T(8,128)(2,1)} async-done(((bf16[128,8,6656]{0,2,1:T(8,128)(2,1)}), bf16[128,8,6656]{0,2,1:T(8,128)(2,1)}, u32[]{:S(2)}, u32[]{:S(2)}) %all-to-all-start) | async-done | bytes 13631520 | tf_op jit(solution)/shard_map/all_to_all | solution.py:43
  182.3 17.5 %copy.17 = bf16[8,128,6656]{2,1,0:T(8,128)(2,1)} copy(bf16[8,128,6656]{1,2,0:T(8,128)(2,1)} %bitcast.2) | data formatting | bytes 27262976 | tf_op jit(solution)/shard_map/all_to_all | solution.py:43
  199.8 7.8 fusion.36
  207.6 6.7 concatenate.9
  214.4 19.4 %while.5 = (s32[]{:T(128)}, bf16[4,256,6656]{2,1,0:T(8,128)(2,1)}, s32[4,3]{1,0:T(4,128)S(1)}, bf16[4,128,6656]{2,1,0:T(8,128)(2,1)}, s32[]{:T(128)}) while((s32[]{:T(128)}, bf16[4,256,6656]{2,1,0:T(8,128)(2,1)}, s32[4,3]{1,0:T(4,128)S(1)}, bf16[4,128,6656]{2,1,0:T(8,128)(2,1)}, s32[]{:T(128)}) %tuple.63), condition=%wide.while_cond.1, body=%wide.while_body.1.sunk | while | flops 2 | bytes 3409513 | solution.py:13
  214.9 4.3 dynamic-slice_dynamic-update-slice_fusion.2
  219.8 4.3 dynamic-slice_dynamic-update-slice_fusion.2
  224.6 4.3 dynamic-slice_dynamic-update-slice_fusion.2
  229.5 4.3 dynamic-slice_dynamic-update-slice_fusion.2
  233.7 8.4 %bitcast_select_fusion = bf16[512,6656]{1,0:T(8,128)(2,1)} fusion(bf16[4,128,6656]{2,1,0:T(8,128)(2,1)} %get-tuple-element.19, bf16[4,1,128,6656]{3,2,1,0:T(8,128)(2,1)} %get-tuple-element.58, pred[512]{0:T(512)(128)(4,1)S(1)} %fusion.30), kind=kLoop, calls=%fused_computation.11 | loop fusion | flops 3407872 | bytes 20447744 | tf_op jit(solution)/shard_map/vmap(jit(_where))/select_n | solution.py:14
  242.2 5.7 convolution_subtract_fusion.2
  248.0 54.7 %all-reduce.9.cloned.1.call-done = f32[512,256]{1,0:T(8,128)} async-done(((f32[512,256]{1,0:T(8,128)}), f32[512,256]{1,0:T(8,128)}) %all-reduce.9.cloned.1.call-update) | async-done | bytes 524304 | tf_op jit(solution)/shard_map/psum | solution.py:57
  302.7 2.9 fusion.38
  306.6 33.8 %all-reduce.11.cloned.1.call-done = f32[256,256]{0,1:T(8,128)} async-done(((f32[256,256]{0,1:T(8,128)}), f32[256,256]{0,1:T(8,128)}) %all-reduce.11.cloned.1.call-update) | async-done | bytes 262160 | tf_op jit(solution)/shard_map/psum | solution.py:58
  340.4 1.8 copy.19
  344.0 11.7 %cholesky.130 = f32[128,128]{1,0:T(8,128)S(1)} custom-call(f32[128,128]{1,0:T(8,128)S(1)} %cholesky.194), custom_call_target="Cholesky" | custom-call | tf_op jit(solution)/shard_map/jit(cholesky)/cholesky | solution.py:18
  355.8 10.4 %custom-call.13 = f32[1,128,128]{1,2,0:T(8,128)} custom-call(f32[1,128,128]{2,1,0:T(8,128)S(1)} %get-tuple-element.67), custom_call_target="InvertDiagBlocksLowerTriangular" | custom-call | tf_op jit(solution)/shard_map/jit(cholesky)/cholesky | solution.py:18
  366.9 1.7 constant_dynamic-update-slice_fusion.3
  369.7 11.7 %cholesky.147 = f32[128,128]{1,0:T(8,128)S(1)} custom-call(f32[128,128]{1,0:T(8,128)S(1)} %convolution_subtract_fusion.6), custom_call_target="Cholesky" | custom-call | tf_op jit(solution)/shard_map/jit(cholesky)/cholesky | solution.py:18
  385.8 5.9 while.6
  386.6 2.3 bitcast_dynamic-update-slice_fusion.4
  389.5 2.2 bitcast_dynamic-update-slice_fusion.4
  392.4 20.5 %custom-call.14 = f32[2,128,128]{1,2,0:T(8,128)S(1)} custom-call(f32[2,128,128]{2,1,0:T(8,128)} %copy-done.5), custom_call_target="InvertDiagBlocksLowerTriangular" | custom-call | tf_op jit(solution)/shard_map/triangular_solve/custom-call.0 | solution.py:20
  415.6 1.8 convolution_convert_fusion
  417.5 5.1 fusion.39
  422.6 4.0 fusion
  426.7 129.4 %all-reduce.13.cloned.1.call-done = bf16[256,6656]{1,0:T(8,128)(2,1)} async-done(((bf16[256,6656]{1,0:T(8,128)(2,1)}), bf16[256,6656]{1,0:T(8,128)(2,1)}) %all-reduce.13.cloned.1.call-update) | async-done | bytes 3407888 | tf_op jit(solution)/shard_map/psum | solution.py:66
  556.1 6.0 fusion.40
  562.1 5.7 fusion.2
  567.9 53.6 %all-reduce.15.cloned.1.call-done = f32[512,256]{0,1:T(8,128)} async-done(((f32[512,256]{0,1:T(8,128)}), f32[512,256]{0,1:T(8,128)}) %all-reduce.15.cloned.1.call-update) | async-done | bytes 524304 | tf_op jit(solution)/shard_map/psum | solution.py:57
  621.5 2.6 fusion.41
  624.6 34.5 %all-reduce.17.cloned.1.call-done = f32[256,256]{0,1:T(8,128)} async-done(((f32[256,256]{0,1:T(8,128)}), f32[256,256]{0,1:T(8,128)}) %all-reduce.17.cloned.1.call-update) | async-done | bytes 262160 | tf_op jit(solution)/shard_map/psum | solution.py:58
  659.1 1.8 copy.22
  662.6 11.7 %cholesky.164 = f32[128,128]{1,0:T(8,128)S(1)} custom-call(f32[128,128]{1,0:T(8,128)S(1)} %cholesky.197), custom_call_target="Cholesky" | custom-call | tf_op jit(solution)/shard_map/jit(cholesky)/cholesky | solution.py:18
  675.1 9.8 %custom-call.15 = f32[1,128,128]{1,2,0:T(8,128)S(1)} custom-call(f32[1,128,128]{2,1,0:T(8,128)S(1)} %get-tuple-element.63), custom_call_target="InvertDiagBlocksLowerTriangular" | custom-call | tf_op jit(solution)/shard_map/jit(cholesky)/cholesky | solution.py:18
  687.7 11.7 %cholesky.181 = f32[128,128]{1,0:T(8,128)S(1)} custom-call(f32[128,128]{1,0:T(8,128)S(1)} %convolution_subtract_fusion.5), custom_call_target="Cholesky" | custom-call | tf_op jit(solution)/shard_map/jit(cholesky)/cholesky | solution.py:18
  704.4 6.0 while.7
  705.3 2.3 bitcast_dynamic-update-slice_fusion.5
  708.3 2.2 bitcast_dynamic-update-slice_fusion.5
  711.1 20.5 %custom-call.16 = f32[2,128,128]{1,2,0:T(8,128)S(1)} custom-call(f32[2,128,128]{2,1,0:T(8,128)} %copy-done.4), custom_call_target="InvertDiagBlocksLowerTriangular" | custom-call | tf_op jit(solution)/shard_map/triangular_solve/custom-call.0 | solution.py:20
  734.4 2.2 fusion.6
  736.6 5.2 fusion.14
  741.9 3.9 fusion.1
  747.3 62.7 %reduce-scatter.2.cloned.1.call-done = bf16[64,6656]{1,0:T(8,128)(2,1)} async-done(((bf16[256,6656]{1,0:T(8,128)(2,1)}), bf16[64,6656]{1,0:T(8,128)(2,1)}) %reduce-scatter.2.cloned.1.call-update) | async-done | bytes 851984 | tf_op jit(solution)/shard_map/reduce_scatter | solution.py:69
  810.1 2.5 convert_element_type.26
  (91 shorter events, 30.8 us)
Async XLA Ops:
  7.2 24.7 %copy-start = (bf16[256,6656]{1,0:T(8,128)(2,1)S(1)}, bf16[256,6656]{1,0:T(8,128)(2,1)}, u32[]{:S(2)}) copy-start(bf16[256,6656]{1,0:T(8,128)(2,1)} %param.9) | copy-start | bytes 10223620
  25.7 5.7 copy-start.7
  25.7 156.5 %all-to-all-start = ((bf16[128,8,6656]{0,2,1:T(8,128)(2,1)}), bf16[128,8,6656]{0,2,1:T(8,128)(2,1)}, u32[]{:S(2)}, u32[]{:S(2)}) async-start(bf16[128,8,6656]{0,2,1:T(8,128)(2,1)} %bitcast.107), calls=%async_computation | async-start | bytes 27262976 | tf_op jit(solution)/shard_map/all_to_all | solution.py:43
  31.3 271.4 %all-reduce.9.cloned.1.call-start = ((), (), s32[]{:S(2)}) async-start(), calls=%async_computation.2 | async-start | bytes 1048576 | tf_op jit(solution)/shard_map/psum | solution.py:57
  247.9 92.5 %all-reduce.11.cloned.1.call-start = ((), (), s32[]{:S(2)}) async-start(), calls=%async_computation.3 | async-start | bytes 524288 | tf_op jit(solution)/shard_map/psum | solution.py:58
  305.7 250.5 %all-reduce.13.cloned.1.call-start = ((), (), s32[]{:S(2)}) async-start(), calls=%async_computation.4 | async-start | bytes 6815744 | tf_op jit(solution)/shard_map/psum | solution.py:66
  343.3 0.7 copy-start.2
  391.7 0.6 copy-start.5
  415.6 7.0 slice-start
  417.5 5.2 slice-start.1
  426.7 194.9 %all-reduce.15.cloned.1.call-start = ((), (), s32[]{:S(2)}) async-start(), calls=%async_computation.5 | async-start | bytes 1048576 | tf_op jit(solution)/shard_map/psum | solution.py:57
  556.1 6.0 copy-start.6
  567.8 91.2 %all-reduce.17.cloned.1.call-start = ((), (), s32[]{:S(2)}) async-start(), calls=%async_computation.6 | async-start | bytes 524288 | tf_op jit(solution)/shard_map/psum | solution.py:58
  624.1 185.9 %reduce-scatter.2.cloned.1.call-start = ((), (), s32[]{:S(2)}) async-start(), calls=%async_computation.7 | async-start | bytes 4259840 | tf_op jit(solution)/shard_map/reduce_scatter | solution.py:69
  661.9 0.7 copy-start.3
  710.5 0.6 copy-start.4
  734.4 7.5 slice-start.2
  736.6 5.2 copy-start.1
  736.6 5.3 slice-start.3
Sparse Core Ops, SparseCore 0:
  248.0 54.6 all-reduce.8
  305.8 34.6 all-reduce.10
  426.8 129.2 all-reduce.12
  568.0 53.5 all-reduce.14
  624.4 34.6 all-reduce.16
  746.0 64.0 reduce-scatter.1
where the time goes:
time: 826 us; the launch traced here: 820 us
  waiting for transfers between devices  514 us (62%)
  other arithmetic  130 us (16%)
  local copies, waits for them, and re-layouts  89.5 us (11%)
  matrix products  61.9 us (7%)
  between operations  17.2 us (2%)
    all_to_all x1, waiting for transfers between devices, per_device(): lax.all_to_all(base_rows, 'col', split_axis=1, concat_axis=0, tiled=True)  145 us
    psum x1, waiting for transfers between devices, per_device(): right_side = lax.psum(projected.astype(jnp.bfloat16), 'row')  129 us
    psum x2, waiting for transfers between devices, per_device(): group_rows = lax.psum(partial_value, 'col')  108 us
    another operation x13, other arithmetic, orthonormal(): factor = jnp.linalg.cholesky(gram_matrix)  70.5 us
    psum x2, waiting for transfers between devices, per_device(): lax.psum(jnp.dot(group_rows.T, group_rows, precision=lax.Precision.HIGHES...  68.3 us
    reduce_scatter x1, waiting for transfers between devices, per_device(): lax.psum_scatter(projected.astype(jnp.bfloat16), 'row', scatter_dimension...  62.7 us
    another operation x5, other arithmetic, orthonormal(): lax.linalg.triangular_solve(factor, identity, left_side=True, lower=True)  44.3 us
    dot_general x4, matrix products, against(): lax.dot_general(left_side, right_side, (((1,), (1,)), ((), ())), preferre...  23.1 us
  transfers between devices with their start and end apart: 7, of which 7 were waited for; matrix products, arithmetic and copies ran while one was open for 1% of the time, Pallas kernels for 0%

commit v1 on v0

v1 whole, which is shorter than its diff:
```python
import functools
import math

import jax
import jax.numpy as jnp
from jax import lax
from jax.experimental import pallas as pl
from jax.experimental.pallas import tpu as pltpu
from jax.sharding import PartitionSpec as P

MESH = pl.DeviceIdType.MESH
HIGHEST = lax.Precision.HIGHEST
VMEM_LIMIT = 58 * 1024 * 1024


def flip(index, mask, count):
    if count & (count - 1):
        raise ValueError("count")
    result, bit = 0, 1
    while bit < count:
        digit = lax.rem(lax.div(index, bit), 2)
        result = result + bit * ((1 - digit) if mask & bit else digit)
        bit *= 2
    return result


def column_tile(width):
    lanes = width // 128
    return 128 * max(d for d in range(1, 9) if lanes % d == 0)


def gather_kernel(
    chips, select, base, fine, test, delta, sketch,
    mine, other, landed, work,
    mine_sem, pair_send, pair_recv, send_sem, recv_sem, fine_sem, delta_sem,
):
    row = lax.axis_index("row")
    col = lax.axis_index("col")
    chip = lax.div(col, 2)
    core = lax.rem(col, 2)
    rows, width = mine.shape[1], mine.shape[2]
    tile = column_tile(width)
    partner = (row, 2 * chip + (1 - core))

    barrier = pltpu.get_barrier_semaphore()
    pl.semaphore_signal(barrier, inc=1, device_id=partner, device_id_type=MESH)
    for o in range(1, chips):
        pl.semaphore_signal(
            barrier, inc=1, device_id=(row, 2 * flip(chip, o, chips) + core), device_id_type=MESH
        )
    pl.semaphore_wait(barrier, chips)

    order = list(range(chips - 1, -1, -1))
    pair, local = {}, {}
    for o in order:
        block = flip(chip, o, chips)
        away = pl.ds(pl.multiple_of((2 * block + (1 - core)) * width, 128), width)
        keep = pl.ds(pl.multiple_of((2 * block + core) * width, 128), width)
        pair[o] = pltpu.make_async_remote_copy(
            src_ref=base.at[:, away], dst_ref=other.at[o],
            send_sem=pair_send.at[o], recv_sem=pair_recv.at[o],
            device_id=partner, device_id_type=MESH,
        )
        pair[o].start()
        local[o] = pltpu.make_async_copy(base.at[:, keep], mine.at[o], mine_sem.at[o])
        local[o].start()
    loads = {}
    for o in order:
        block = flip(chip, o, chips)
        here = pl.ds(pl.multiple_of(block * rows, rows), rows)
        loads[o] = pltpu.make_async_copy(fine.at[here, :], work.at[o], fine_sem.at[o])
        loads[o].start()

    sends = {}
    for o in order:
        local[o].wait()
        pair[o].wait_recv()

        @pl.loop(0, width // tile)
        def compose(step):
            at = pl.ds(pl.multiple_of(step * tile, 128), tile)
            merged = jnp.dot(select[0], mine[o, :, at], preferred_element_type=jnp.float32)
            merged += jnp.dot(select[1], other[o, :, at], preferred_element_type=jnp.float32)
            mine[o, :, at] = merged.astype(jnp.bfloat16)

        if o:
            sends[o] = pltpu.make_async_remote_copy(
                src_ref=mine.at[o], dst_ref=landed.at[o],
                send_sem=send_sem.at[o], recv_sem=recv_sem.at[o],
                device_id=(row, 2 * flip(chip, o, chips) + core), device_id_type=MESH,
            )
            sends[o].start()

    stores = []
    for o in [0] + order[:-1]:
        block = flip(chip, o, chips)
        here = pl.ds(pl.multiple_of(block * rows, rows), rows)
        if o:
            sends[o].wait_recv()
        loads[o].wait()
        source = landed if o else mine

        def difference(step, total):
            at = pl.ds(pl.multiple_of(step * tile, 128), tile)
            value = work[o, :, at].astype(jnp.float32) - source[o, :, at].astype(jnp.float32)
            value = value.astype(jnp.bfloat16)
            work[o, :, at] = value
            return total + lax.dot_general(
                value, test[:, at], (((1,), (1,)), ((), ())), preferred_element_type=jnp.float32
            )

        total = lax.fori_loop(
            0, width // tile, difference, jnp.zeros((rows, test.shape[0]), jnp.float32)
        )
        sketch[here, :] = total
        store = pltpu.make_async_copy(work.at[o], delta.at[here, :], delta_sem.at[o])
        store.start()
        stores.append(store)
    for store in stores:
        store.wait()
    for o in order:
        pair[o].wait_send()
        if o:
            sends[o].wait_send()


def sum_kernel(
    col_count, row_count, partial, full, gram,
    arrived, local_gram, crossed,
    a_send, a_recv, b_send, b_recv, c_send, c_recv, d_send, d_recv,
):
    row = lax.axis_index("row")
    col = lax.axis_index("col")
    own_rows = arrived.shape[1]
    gram_rows = crossed.shape[1]

    def peer(o):
        return lax.rem(col + o, col_count)

    def above(o):
        return lax.rem(row + o, row_count)

    barrier = pltpu.get_barrier_semaphore()
    for o in range(1, col_count):
        pl.semaphore_signal(barrier, inc=1, device_id=(row, peer(o)), device_id_type=MESH)
    for o in range(1, row_count):
        pl.semaphore_signal(barrier, inc=1, device_id=(above(o), col), device_id_type=MESH)
    pl.semaphore_wait(barrier, col_count + row_count - 2)

    own = pl.ds(pl.multiple_of(col * own_rows, own_rows), own_rows)
    strip = pl.ds(pl.multiple_of(col * gram_rows, gram_rows), gram_rows)

    def copy(source, target, send, recv, o, device):
        made = pltpu.make_async_remote_copy(
            src_ref=source, dst_ref=target, send_sem=send.at[o], recv_sem=recv.at[o],
            device_id=device, device_id_type=MESH,
        )
        made.start()
        return made

    first = []
    for o in range(1, col_count):
        theirs = pl.ds(pl.multiple_of(peer(o) * own_rows, own_rows), own_rows)
        first.append(
            copy(partial.at[theirs, :], arrived.at[o], a_send, a_recv, o, (row, peer(o)))
        )
    total = partial[own, :]
    for o in range(1, col_count):
        first[o - 1].wait_recv()
        total = total + arrived[o]
    full[own, :] = total
    second = [
        copy(full.at[own, :], full.at[own, :], b_send, b_recv, o, (row, peer(o)))
        for o in range(1, col_count)
    ]
    for made in second:
        made.wait_recv()
    local_gram[...] = lax.dot_general(
        full[...], full[...], (((0,), (0,)), ((), ())),
        precision=HIGHEST, preferred_element_type=jnp.float32,
    )
    third = [
        copy(local_gram.at[strip, :], crossed.at[o], c_send, c_recv, o, (above(o), col))
        for o in range(1, row_count)
    ]
    total = local_gram[strip, :]
    for o in range(1, row_count):
        third[o - 1].wait_recv()
        total = total + crossed[o]
    gram[strip, :] = total
    fourth = [
        copy(gram.at[strip, :], gram.at[strip, :], d_send, d_recv, o, (row, peer(o)))
        for o in range(1, col_count)
    ]
    for made in fourth:
        made.wait_recv()
    for made in first + second + third + fourth:
        made.wait_send()


def factor_kernel(panel, scale, full, gram, own, narrow, basis, table):
    size = gram.shape[0]
    table[:, :size] = gram[...]
    row_ids = lax.broadcasted_iota(jnp.int32, (size, size), 0)
    column_ids = lax.broadcasted_iota(jnp.int32, (size, size), 1)
    table[:, size:] = (row_ids == column_ids).astype(jnp.float32)
    for start in range(0, size, panel):
        low = start // 128 * 128
        high = size + low + 128
        block = table[start:start + panel, low:high]
        ids = lax.broadcasted_iota(jnp.int32, (panel, 1), 0)
        pivots = jnp.ones((panel, 1), jnp.float32)
        for i in range(panel):
            at = start + i - low
            column = block[:, at:at + 1]
            line = block[i:i + 1, :]
            pivot = column[i:i + 1, :]
            pivots = jnp.where(ids == i, pivot, pivots)
            if i + 1 < panel:
                weight = jnp.where(ids > i, column * (1.0 / pivot), 0.0)
                block = block - weight * line
        block = block * (1.0 / jnp.sqrt(pivots))
        table[start:start + panel, low:high] = block
        end = start + panel
        if end < size:
            update = lax.dot_general(
                block[:, :size - low], block, (((0,), (0,)), ((), ())),
                precision=HIGHEST, preferred_element_type=jnp.float32,
            )
            table[end:, low:high] = table[end:, low:high] - update[end - low:, :]
    inverse = table[:, size:]
    inverse = jnp.where(column_ids <= row_ids, inverse, 0.0)

    def apply(rows):
        return lax.dot_general(
            rows, inverse, (((1,), (1,)), ((), ())),
            precision=HIGHEST, preferred_element_type=jnp.float32,
        )

    narrow[...] = apply(full[...]).astype(jnp.bfloat16)
    basis[...] = apply(own[...]) * scale


def vmem():
    return pl.BlockSpec(memory_space=pltpu.VMEM)


def anywhere():
    return pl.BlockSpec(memory_space=pl.ANY)


def gather(select, base_rows, finetune, test_matrix, chips):
    capacity = base_rows.shape[0]
    rows, width = finetune.shape
    sketch_size = test_matrix.shape[0]
    slots = pltpu.VMEM((chips, capacity, width), jnp.bfloat16)
    sems = pltpu.SemaphoreType.DMA((chips,))
    return pl.pallas_call(
        functools.partial(gather_kernel, chips),
        out_shape=(
            jax.ShapeDtypeStruct((rows, width), jnp.bfloat16),
            jax.ShapeDtypeStruct((rows, sketch_size), jnp.float32),
        ),
        in_specs=[vmem(), anywhere(), anywhere(), vmem()],
        out_specs=(anywhere(), vmem()),
        scratch_shapes=[slots] * 4 + [sems] * 7,
        compiler_params=pltpu.CompilerParams(
            collective_id=0, has_side_effects=True, vmem_limit_bytes=VMEM_LIMIT
        ),
        cost_estimate=pl.CostEstimate(
            flops=2 * rows * width * sketch_size, bytes_accessed=8 * rows * width, transcendentals=0
        ),
    )(select, base_rows, finetune, test_matrix)


def group_sums(partial, col_count, row_count, collective_id):
    rows, size = partial.shape
    col_sems = pltpu.SemaphoreType.DMA((col_count,))
    row_sems = pltpu.SemaphoreType.DMA((row_count,))
    return pl.pallas_call(
        functools.partial(sum_kernel, col_count, row_count),
        out_shape=(
            jax.ShapeDtypeStruct((rows, size), jnp.float32),
            jax.ShapeDtypeStruct((size, size), jnp.float32),
        ),
        in_specs=[vmem()],
        out_specs=(vmem(), vmem()),
        scratch_shapes=[
            pltpu.VMEM((col_count, rows // col_count, size), jnp.float32),
            pltpu.VMEM((size, size), jnp.float32),
            pltpu.VMEM((row_count, size // col_count, size), jnp.float32),
            col_sems, col_sems, col_sems, col_sems,
            row_sems, row_sems, col_sems, col_sems,
        ],
        compiler_params=pltpu.CompilerParams(
            collective_id=collective_id, has_side_effects=True, vmem_limit_bytes=VMEM_LIMIT
        ),
    )(partial)


def orthonormal(full, gram, own, scale):
    rows, size = full.shape
    return pl.pallas_call(
        functools.partial(factor_kernel, 32, scale),
        out_shape=(
            jax.ShapeDtypeStruct((rows, size), jnp.bfloat16),
            jax.ShapeDtypeStruct(own.shape, jnp.float32),
        ),
        in_specs=[vmem()] * 3,
        out_specs=(vmem(), vmem()),
        scratch_shapes=[pltpu.VMEM((size, 2 * size), jnp.float32)],
        compiler_params=pltpu.CompilerParams(vmem_limit_bytes=VMEM_LIMIT),
    )(full, gram, own)


def per_device(finetune, base_rows, test_matrix, base_lengths):
    col_count = lax.axis_size("col")
    row_count = lax.axis_size("row")
    col = lax.axis_index("col")
    row = lax.axis_index("row")
    capacity = base_rows.shape[0]
    chips = col_count // 2
    group = finetune.shape[0]
    total_rows = group * row_count
    own_rows = group // col_count

    first_count = lax.dynamic_index_in_dim(
        base_lengths, row * col_count + col // 2 * 2, 0, keepdims=False
    )
    slab_row = jnp.arange(capacity)[:, None]
    slot = jnp.arange(capacity)[None, :]
    from_first = (slab_row == slot) & (slab_row < first_count)
    from_second = slab_row - first_count == slot
    is_first = col % 2 == 0
    select = jnp.stack(
        [jnp.where(is_first, from_first, from_second), jnp.where(is_first, from_second, from_first)]
    ).astype(jnp.bfloat16)

    delta, partial = gather(select, base_rows, finetune, test_matrix, chips)
    for sweep in range(2):
        full, gram = group_sums(partial, col_count, row_count, 1 + sweep)
        own = lax.dynamic_slice_in_dim(full, col * own_rows, own_rows, 0)
        narrow, basis = orthonormal(full, gram, own, math.sqrt(total_rows))
        projected = lax.dot_general(
            narrow, delta, (((0,), (0,)), ((), ())), preferred_element_type=jnp.float32
        ).astype(jnp.bfloat16)
        if sweep == 0:
            right_side = lax.psum(projected, "row")
            partial = lax.dot_general(
                delta, right_side, (((1,), (1,)), ((), ())), preferred_element_type=jnp.float32
            )
    coefficients = lax.psum_scatter(
        projected, "row", scatter_dimension=0, tiled=True
    ).astype(jnp.float32)
    return (basis, coefficients)


def solution(mesh):
    return jax.shard_map(
        per_device,
        mesh=mesh,
        in_specs=(P("row", "col"), P(("row", "col"), None), P(None, "col"), P()),
        out_specs=(P(("row", "col"), None), P("row", "col")),
        check_vma=False,
    )
```

time: 826 us -> 446 us (0.54)
  waiting for transfers between devices: 514 us -> 193 us
  Pallas kernels: 0 us -> 209 us
  other arithmetic: 130 us -> 4.5 us
  local copies, waits for them, and re-layouts: 89.5 us -> 4.2 us
  matrix products: 61.9 us -> 20.2 us
    pallas_call x0 -> x5, Pallas kernels: none -> 209 us  [the longest x1 94.9 us: gather(): pl.pallas_call(functools.partial(gather_kernel, chips), out_shape=(jax.Sh...]
    psum x5 -> x1, waiting for transfers between devices: 306 us -> 129 us  [per_device(): right_side = lax.psum(projected, 'row')]
    all_to_all x1 -> x0, waiting for transfers between devices: 145 us -> none  [per_device(): lax.all_to_all(base_rows, 'col', split_axis=1, concat_axis=0, tiled=True)]
    another operation x18 -> x0, other arithmetic: 115 us -> none  [the longest x13 70.5 us: orthonormal(): factor = jnp.linalg.cholesky(gram_matrix)]
    dot_general x12 -> x3, matrix products: 50.9 us -> 20.2 us  [the longest x2 13.6 us: per_device(): lax.dot_general(narrow, delta, (((0,), (0,)), ((), ())), preferred_elemen...]
    unnamed x26 -> x0, local copies, waits for them, and re-layouts: 21.3 us -> none
    gather x12 -> x0, local copies, waits for them, and re-layouts: 19.4 us -> none
    all_to_all x1 -> x0, local copies, waits for them, and re-layouts: 17.5 us -> none  [per_device(): lax.all_to_all(base_rows, 'col', split_axis=1, concat_axis=0, tiled=True)]
  transfers between devices with their start and end apart: 7 -> 2, of which waited for: 7 -> 2; matrix products, arithmetic and copies ran while one was open for 1% -> 0% of each run, Pallas kernels for 0% -> 0%
where the time goes in v1:
time: 446 us
  Pallas kernels  209 us (47%)
  waiting for transfers between devices  193 us (43%)
  matrix products  20.2 us (5%)
  between operations  14.1 us (3%)
  other arithmetic  4.5 us (1%)
    psum x1, waiting for transfers between devices, per_device(): right_side = lax.psum(projected, 'row')  129 us
    pallas_call x1, Pallas kernels, gather(): pl.pallas_call(functools.partial(gather_kernel, chips), out_shape=(jax.Sh...  94.9 us
    reduce_scatter x1, waiting for transfers between devices, per_device(): lax.psum_scatter(projected, 'row', scatter_dimension=0, tiled=True)  63.9 us
    pallas_call x2, Pallas kernels, group_sums(): pl.pallas_call(functools.partial(sum_kernel, col_count, row_count), out_s...  58.4 us
    pallas_call x2, Pallas kernels, orthonormal(): pl.pallas_call(functools.partial(factor_kernel, 32, scale), out_shape=(ja...  55.8 us
    dot_general x2, matrix products, per_device(): lax.dot_general(narrow, delta, (((0,), (0,)), ((), ())), preferred_elemen...  13.6 us
  transfers between devices with their start and end apart: 2, of which 2 were waited for; matrix products, arithmetic and copies ran while one was open for 0% of the time, Pallas kernels for 0%

profile of v1, /device:TPU:0, one launch (start us, length us, event | category | flops | bytes accessed | tf_op | source)
XLA Modules:
  0.0 445.7 jit_solution(4646108755023462581)
XLA Ops:
  7.2 0.0 all-reduce.2.cloned.1.call-start
  7.2 1.2 dynamic_slice.10
  8.5 0.6 iota_subtract_fusion
  9.1 0.7 iota_compare_fusion.2
  9.8 0.1 fusion.1
  9.9 0.6 add_convert_fusion.select
  10.6 94.9 %shard_map.59 = (bf16[512,6656]{1,0:T(8,128)(2,1)}, f32[512,256]{1,0:T(8,128)}) custom-call(bf16[2,128,128]{2,1,0:T(8,128)(2,1)} %add_convert_fusion.select, bf16[128,53248]{1,0:T(8,128)(2,1)} %base.1, bf16[512,6656]{1,0:T(8,128)(2,1)} %fine.1, bf16[256,6656]{1,0:T(8,128)(2,1)} %test.1), custom_call_target="tpu_custom_call" | custom-call | flops 1744830464 | bytes 27262976 | tf_op jit(solution)/shard_map/pallas_call | solution.py:258
  105.5 29.9 %shard_map.60 = (f32[512,256]{1,0:T(8,128)}, f32[256,256]{1,0:T(8,128)}) custom-call(f32[512,256]{1,0:T(8,128)} %get-tuple-element.12.partial), custom_call_target="tpu_custom_call" | custom-call | tf_op jit(solution)/shard_map/pallas_call | solution.py:280
  135.4 1.5 constant_dynamic-slice_fusion.1.own
  136.8 27.9 %shard_map.61 = (bf16[512,256]{1,0:T(8,128)(2,1)}, f32[64,256]{1,0:T(8,128)}) custom-call(f32[512,256]{1,0:T(8,128)} %get-tuple-element.13.full, f32[256,256]{1,0:T(8,128)} %get-tuple-element.14.gram, f32[64,256]{1,0:T(8,128)} %constant_dynamic-slice_fusion.1.own), custom_call_target="tpu_custom_call" | custom-call | tf_op jit(solution)/shard_map/pallas_call | solution.py:303
  164.7 6.8 %convolution_convert_fusion.1 = bf16[256,6656]{1,0:T(8,128)(2,1)} fusion(bf16[512,256]{1,0:T(8,128)(2,1)} %get-tuple-element.15, bf16[512,6656]{1,0:T(8,128)(2,1)} %get-tuple-element.11), kind=kOutput, calls=%fused_computation.1 | convolution fusion | flops 1746534400 | bytes 10485760 | tf_op jit(solution)/shard_map/dot_general | solution.py:344
  171.5 0.0 all-reduce.2.cloned.1.call-update
  171.6 0.2 reduce-scatter.2.cloned.1.call-start
  171.8 129.4 %all-reduce.2.cloned.1.call-done = bf16[256,6656]{1,0:T(8,128)(2,1)} async-done(((bf16[256,6656]{1,0:T(8,128)(2,1)}), bf16[256,6656]{1,0:T(8,128)(2,1)}) %all-reduce.2.cloned.1.call-update) | async-done | bytes 3407888 | tf_op jit(solution)/shard_map/psum | solution.py:348
  301.1 6.6 %fusion.3.partial = f32[512,256]{1,0:T(8,128)} fusion(bf16[512,6656]{1,0:T(8,128)(2,1)} %get-tuple-element.11, bf16[256,6656]{1,0:T(8,128)(2,1)} %all-reduce.2.cloned.1.call-done), kind=kOutput, calls=%fused_computation.12 | convolution fusion | flops 1744830464 | bytes 10747904 | tf_op jit(solution)/shard_map/dot_general | solution.py:349
  307.8 28.5 %shard_map.62 = (f32[512,256]{1,0:T(8,128)}, f32[256,256]{1,0:T(8,128)}) custom-call(f32[512,256]{1,0:T(8,128)} %fusion.3.partial), custom_call_target="tpu_custom_call" | custom-call | tf_op jit(solution)/shard_map/pallas_call | solution.py:280
  336.3 1.5 constant_dynamic-slice_fusion.own
  337.8 27.9 %shard_map.63 = (bf16[512,256]{1,0:T(8,128)(2,1)}, f32[64,256]{1,0:T(8,128)}) custom-call(f32[512,256]{1,0:T(8,128)} %get-tuple-element.16.full, f32[256,256]{1,0:T(8,128)} %get-tuple-element.17.gram, f32[64,256]{1,0:T(8,128)} %constant_dynamic-slice_fusion.own), custom_call_target="tpu_custom_call" | custom-call | tf_op jit(solution)/shard_map/pallas_call | solution.py:303
  365.7 6.8 %convolution_convert_fusion = bf16[256,6656]{1,0:T(8,128)(2,1)} fusion(bf16[512,256]{1,0:T(8,128)(2,1)} %get-tuple-element.19, bf16[512,6656]{1,0:T(8,128)(2,1)} %get-tuple-element.11), kind=kOutput, calls=%fused_computation | convolution fusion | flops 1746534400 | bytes 10485760 | tf_op jit(solution)/shard_map/dot_general | solution.py:344
  372.4 0.0 reduce-scatter.2.cloned.1.call-update
  372.5 63.9 %reduce-scatter.2.cloned.1.call-done = bf16[64,6656]{1,0:T(8,128)(2,1)} async-done(((bf16[256,6656]{1,0:T(8,128)(2,1)}), bf16[64,6656]{1,0:T(8,128)(2,1)}) %reduce-scatter.2.cloned.1.call-update) | async-done | bytes 851984 | tf_op jit(solution)/shard_map/reduce_scatter | solution.py:352
  436.4 2.5 convert_element_type.15
Async XLA Ops:
  7.2 294.0 %all-reduce.2.cloned.1.call-start = ((), (), s32[]{:S(2)}) async-start(), calls=%async_computation.1 | async-start | bytes 6815744 | tf_op jit(solution)/shard_map/psum | solution.py:348
  171.6 264.8 %reduce-scatter.2.cloned.1.call-start = ((), (), s32[]{:S(2)}) async-start(), calls=%async_computation.2 | async-start | bytes 4259840 | tf_op jit(solution)/shard_map/reduce_scatter | solution.py:352
Sparse Core Ops, SparseCore 0:
  171.7 129.4 all-reduce.1
  372.6 63.7 reduce-scatter.1

commit v2 on v1

--- a/solution.py
+++ b/solution.py
@@ -39,7 +39,8 @@
     chip = lax.div(col, 2)
     core = lax.rem(col, 2)
     rows, width = mine.shape[1], mine.shape[2]
-    tile = column_tile(width)
+    pieces = mine_sem.shape[1]
+    tile = width // pieces
     partner = (row, 2 * chip + (1 - core))
 
     barrier = pltpu.get_barrier_semaphore()
@@ -50,78 +51,107 @@
         )
     pl.semaphore_wait(barrier, chips)
 
-    order = list(range(chips - 1, -1, -1))
-    pair, local = {}, {}
-    for o in order:
-        block = flip(chip, o, chips)
-        away = pl.ds(pl.multiple_of((2 * block + (1 - core)) * width, 128), width)
-        keep = pl.ds(pl.multiple_of((2 * block + core) * width, 128), width)
-        pair[o] = pltpu.make_async_remote_copy(
-            src_ref=base.at[:, away], dst_ref=other.at[o],
-            send_sem=pair_send.at[o], recv_sem=pair_recv.at[o],
+    far = list(range(chips - 1, 0, -1))
+
+    def columns(q):
+        return pl.ds(pl.multiple_of(q * tile, 128), tile)
+
+    def rows_of(o):
+        return pl.ds(pl.multiple_of(flip(chip, o, chips) * rows, rows), rows)
+
+    def source(o, q, side):
+        start = (2 * flip(chip, o, chips) + side) * width + q * tile
+        return base.at[:, pl.ds(pl.multiple_of(start, 128), tile)]
+
+    def pair(o, q):
+        return pltpu.make_async_remote_copy(
+            src_ref=source(o, q, 1 - core), dst_ref=other.at[o, :, columns(q)],
+            send_sem=pair_send.at[o, q], recv_sem=pair_recv.at[o, q],
             device_id=partner, device_id_type=MESH,
         )
-        pair[o].start()
-        local[o] = pltpu.make_async_copy(base.at[:, keep], mine.at[o], mine_sem.at[o])
-        local[o].start()
-    loads = {}
-    for o in order:
-        block = flip(chip, o, chips)
-        here = pl.ds(pl.multiple_of(block * rows, rows), rows)
-        loads[o] = pltpu.make_async_copy(fine.at[here, :], work.at[o], fine_sem.at[o])
-        loads[o].start()
-
-    sends = {}
-    for o in order:
-        local[o].wait()
-        pair[o].wait_recv()
-
-        @pl.loop(0, width // tile)
-        def compose(step):
-            at = pl.ds(pl.multiple_of(step * tile, 128), tile)
-            merged = jnp.dot(select[0], mine[o, :, at], preferred_element_type=jnp.float32)
-            merged += jnp.dot(select[1], other[o, :, at], preferred_element_type=jnp.float32)
-            mine[o, :, at] = merged.astype(jnp.bfloat16)
-
-        if o:
-            sends[o] = pltpu.make_async_remote_copy(
-                src_ref=mine.at[o], dst_ref=landed.at[o],
-                send_sem=send_sem.at[o], recv_sem=recv_sem.at[o],
-                device_id=(row, 2 * flip(chip, o, chips) + core), device_id_type=MESH,
-            )
-            sends[o].start()
-
-    stores = []
-    for o in [0] + order[:-1]:
-        block = flip(chip, o, chips)
-        here = pl.ds(pl.multiple_of(block * rows, rows), rows)
-        if o:
-            sends[o].wait_recv()
-        loads[o].wait()
-        source = landed if o else mine
-
-        def difference(step, total):
-            at = pl.ds(pl.multiple_of(step * tile, 128), tile)
-            value = work[o, :, at].astype(jnp.float32) - source[o, :, at].astype(jnp.float32)
-            value = value.astype(jnp.bfloat16)
-            work[o, :, at] = value
-            return total + lax.dot_general(
-                value, test[:, at], (((1,), (1,)), ((), ())), preferred_element_type=jnp.float32
-            )
-
-        total = lax.fori_loop(
-            0, width // tile, difference, jnp.zeros((rows, test.shape[0]), jnp.float32)
-        )
-        sketch[here, :] = total
-        store = pltpu.make_async_copy(work.at[o], delta.at[here, :], delta_sem.at[o])
-        store.start()
-        stores.append(store)
-    for store in stores:
-        store.wait()
-    for o in order:
-        pair[o].wait_send()
-        if o:
-            sends[o].wait_send()
+
+    def keep(o, q):
+        return pltpu.make_async_copy(
+            source(o, q, core), mine.at[o, :, columns(q)], mine_sem.at[o, q]
+        )
+
+    def load(o):
+        return pltpu.make_async_copy(fine.at[rows_of(o), :], work.at[o], fine_sem.at[o])
+
+    def send(o, q):
+        return pltpu.make_async_remote_copy(
+            src_ref=mine.at[o, :, columns(q)], dst_ref=landed.at[o, :, columns(q)],
+            send_sem=send_sem.at[o, q], recv_sem=recv_sem.at[o, q],
+            device_id=(row, 2 * flip(chip, o, chips) + core), device_id_type=MESH,
+        )
+
+    def store(o, q):
+        return pltpu.make_async_copy(
+            work.at[o, :, columns(q)], delta.at[rows_of(o), columns(q)], delta_sem.at[o, q]
+        )
+
+    def compose(o, q):
+        keep(o, q).wait()
+        pair(o, q).wait_recv()
+        merged = jnp.dot(
+            select[0], mine[o, :, columns(q)], preferred_element_type=jnp.float32
+        ) + jnp.dot(
+            select[1], other[o, :, columns(q)], preferred_element_type=jnp.float32
+        )
+        mine[o, :, columns(q)] = merged.astype(jnp.bfloat16)
+
+    def difference(o, q, composed):
+        value = work[o, :, columns(q)].astype(jnp.float32)
+        value = (value - composed[o, :, columns(q)].astype(jnp.float32)).astype(jnp.bfloat16)
+        work[o, :, columns(q)] = value
+        store(o, q).start()
+        sketch[rows_of(o), :] += lax.dot_general(
+            value, test[:, columns(q)], (((1,), (1,)), ((), ())),
+            preferred_element_type=jnp.float32,
+        )
+
+    @pl.loop(0, pieces)
+    def start_far(q):
+        for o in far:
+            pair(o, q).start()
+            keep(o, q).start()
+
+    @pl.loop(0, pieces)
+    def start_near(q):
+        pair(0, q).start()
+        keep(0, q).start()
+
+    for o in [0] + far:
+        load(o).start()
+    sketch[...] = jnp.zeros_like(sketch)
+
+    @pl.loop(0, pieces)
+    def send_far(q):
+        for o in far:
+            compose(o, q)
+            send(o, q).start()
+
+    for o in [0] + far:
+        load(o).wait()
+
+    @pl.loop(0, pieces)
+    def finish_near(q):
+        compose(0, q)
+        difference(0, q, mine)
+
+    @pl.loop(0, pieces)
+    def finish_far(q):
+        for o in far:
+            send(o, q).wait_recv()
+            difference(o, q, landed)
+
+    @pl.loop(0, pieces)
+    def drain(q):
+        for o in [0] + far:
+            store(o, q).wait()
+            pair(o, q).wait_send()
+        for o in far:
+            send(o, q).wait_send()
 
 
 def sum_kernel(
@@ -200,25 +230,37 @@
 
 def factor_kernel(panel, scale, full, gram, own, narrow, basis, table):
     size = gram.shape[0]
-    table[:, :size] = gram[...]
     row_ids = lax.broadcasted_iota(jnp.int32, (size, size), 0)
     column_ids = lax.broadcasted_iota(jnp.int32, (size, size), 1)
-    table[:, size:] = (row_ids == column_ids).astype(jnp.float32)
+    eye = row_ids == column_ids
+    diagonal = jnp.where(eye, gram[...], 0.0)
+    scale_rows = 1.0 / jnp.sqrt(jnp.sum(diagonal, axis=1, keepdims=True))
+    scale_columns = 1.0 / jnp.sqrt(jnp.sum(diagonal, axis=0, keepdims=True))
+    table[:, :size] = gram[...] * scale_rows * scale_columns
+    table[:, size:] = eye.astype(jnp.float32)
     for start in range(0, size, panel):
         low = start // 128 * 128
         high = size + low + 128
         block = table[start:start + panel, low:high]
         ids = lax.broadcasted_iota(jnp.int32, (panel, 1), 0)
         pivots = jnp.ones((panel, 1), jnp.float32)
-        for i in range(panel):
+        for i in range(0, panel, 2):
             at = start + i - low
-            column = block[:, at:at + 1]
-            line = block[i:i + 1, :]
-            pivot = column[i:i + 1, :]
+            first, second = block[:, at:at + 1], block[:, at + 1:at + 2]
+            line, next_line = block[i:i + 1, :], block[i + 1:i + 2, :]
+            pivot, cross = first[i:i + 1, :], first[i + 1:i + 2, :]
+            determinant = pivot * second[i + 1:i + 2, :] - cross * cross
+            inverse_pivot = 1.0 / pivot
+            weight = first * inverse_pivot
+            next_weight = (second - weight * cross) * (pivot * (1.0 / determinant))
+            next_line = next_line - (cross * inverse_pivot) * line
             pivots = jnp.where(ids == i, pivot, pivots)
-            if i + 1 < panel:
-                weight = jnp.where(ids > i, column * (1.0 / pivot), 0.0)
-                block = block - weight * line
+            pivots = jnp.where(ids == i + 1, determinant * inverse_pivot, pivots)
+            block = (
+                block
+                - jnp.where(ids > i, weight, 0.0) * line
+                - jnp.where(ids > i + 1, next_weight, 0.0) * next_line
+            )
         block = block * (1.0 / jnp.sqrt(pivots))
         table[start:start + panel, low:high] = block
         end = start + panel
@@ -229,16 +271,219 @@
             )
             table[end:, low:high] = table[end:, low:high] - update[end - low:, :]
     inverse = table[:, size:]
-    inverse = jnp.where(column_ids <= row_ids, inverse, 0.0)
-
-    def apply(rows):
-        return lax.dot_general(
-            rows, inverse, (((1,), (1,)), ((), ())),
-            precision=HIGHEST, preferred_element_type=jnp.float32,
-        )
-
-    narrow[...] = apply(full[...]).astype(jnp.bfloat16)
-    basis[...] = apply(own[...]) * scale
+    inverse = jnp.where(column_ids <= row_ids, inverse * scale_columns, 0.0)
+
+    turned = lax.dot_general(
+        inverse, full[...], (((1,), (1,)), ((), ())),
+        precision=HIGHEST, preferred_element_type=jnp.float32,
+    )
+    narrow[...] = turned.astype(jnp.bfloat16)
+    basis[...] = lax.dot_general(
+        own[...], inverse, (((1,), (1,)), ((), ())),
+        precision=HIGHEST, preferred_element_type=jnp.float32,
+    ) * scale
+
+
+def greet_line(row, row_count, col):
+    barrier = pltpu.get_barrier_semaphore()
+
+    @pl.when(row > 0)
+    def greet_below():
+        pl.semaphore_signal(barrier, inc=1, device_id=(row - 1, col), device_id_type=MESH)
+
+    @pl.when(row < row_count - 1)
+    def greet_above():
+        pl.semaphore_signal(barrier, inc=1, device_id=(row + 1, col), device_id_type=MESH)
+
+    @pl.when((row > 0) & (row < row_count - 1))
+    def hear_both():
+        pl.semaphore_wait(barrier, 2)
+
+    @pl.when((row == 0) | (row == row_count - 1))
+    def hear_one():
+        pl.semaphore_wait(barrier, 1)
+
+
+def resketch_kernel(
+    row_count, narrow, delta, sketch,
+    outbox, inbox, result,
+    up_send, up_recv, down_send, down_recv,
+):
+    row = lax.axis_index("row")
+    col = lax.axis_index("col")
+    pieces, tile = result.shape[0], result.shape[2]
+    root = row_count // 2
+    side = lax.div(row, root + 1)
+    toward = row + 1 - 2 * side
+    away = row - 1 + 2 * side
+    is_root = row == root
+    is_leaf = (row == 0) | ((row == row_count - 1) & (row != root))
+    is_middle = jnp.logical_not(is_root | is_leaf)
+    root_has_above = root < row_count - 1
+
+    greet_line(row, row_count, col)
+    sketch[...] = jnp.zeros_like(sketch)
+
+    def remote(source, target, send, recv, to):
+        return pltpu.make_async_remote_copy(
+            src_ref=source, dst_ref=target, send_sem=send, recv_sem=recv,
+            device_id=(to, col), device_id_type=MESH,
+        )
+
+    def inward(t, lane):
+        return remote(
+            outbox.at[t], inbox.at[lane, t], up_send.at[t], up_recv.at[lane, t], toward
+        )
+
+    def outward(t, lane, to):
+        return remote(
+            result.at[t], result.at[t], down_send.at[lane, t], down_recv.at[t], to
+        )
+
+    def gather_piece(t):
+        at = pl.ds(pl.multiple_of(t * tile, tile), tile)
+        own = jnp.dot(narrow[...], delta[:, at], preferred_element_type=jnp.float32)
+
+        @pl.when(is_leaf)
+        def leaf():
+            outbox[t] = own.astype(jnp.bfloat16)
+            inward(t, side).start()
+
+        @pl.when(is_middle)
+        def middle():
+            inward(t, side).wait_recv()
+            outbox[t] = (own + inbox[side, t].astype(jnp.float32)).astype(jnp.bfloat16)
+            inward(t, side).start()
+
+        @pl.when(is_root)
+        def centre():
+            inward(t, 0).wait_recv()
+            total = own + inbox[0, t].astype(jnp.float32)
+            if root_has_above:
+                inward(t, 1).wait_recv()
+                total = total + inbox[1, t].astype(jnp.float32)
+            result[t] = total.astype(jnp.bfloat16)
+            outward(t, 0, root - 1).start()
+            if root_has_above:
+                outward(t, 1, root + 1).start()
+
+    def return_piece(t):
+        at = pl.ds(pl.multiple_of(t * tile, tile), tile)
+
+        @pl.when(jnp.logical_not(is_root))
+        def arrive():
+            outward(t, 0, toward).wait_recv()
+
+        @pl.when(is_middle)
+        def forward():
+            outward(t, 0, away).start()
+
+        sketch[...] += lax.dot_general(
+            delta[:, at], result[t], (((1,), (1,)), ((), ())),
+            preferred_element_type=jnp.float32,
+        )
+
+    lag = jnp.where(is_leaf, pieces, jnp.where(is_root, 0, min(4, pieces)))
+
+    @pl.loop(0, 2 * pieces)
+    def run(t):
+        @pl.when(t < pieces)
+        def ahead():
+            gather_piece(t)
+
+        @pl.when((t >= lag) & (t < pieces + lag))
+        def behind():
+            return_piece(t - lag)
+
+    @pl.loop(0, pieces)
+    def drain(t):
+        @pl.when(jnp.logical_not(is_root))
+        def sent():
+            inward(t, side).wait_send()
+
+        @pl.when(jnp.logical_not(is_leaf))
+        def returned():
+            outward(t, 0, away).wait_send()
+
+        if root_has_above:
+            @pl.when(is_root)
+            def returned_above():
+                outward(t, 1, root + 1).wait_send()
+
+
+def scatter_kernel(
+    row_count, narrow, delta, coefficients,
+    own, outbox, inbox, send_sem, recv_sem,
+):
+    row = lax.axis_index("row")
+    col = lax.axis_index("col")
+    pieces, block, tile = outbox.shape[2], outbox.shape[3], outbox.shape[4]
+    near = lax.div(2 * row, row_count)
+
+    greet_line(row, row_count, col)
+
+    def columns(t):
+        return pl.ds(pl.multiple_of(t * tile, 128), tile)
+
+    def rows(index):
+        return pl.ds(pl.multiple_of(index * block, block), block)
+
+    def move(way, index, t, to):
+        return pltpu.make_async_remote_copy(
+            src_ref=outbox.at[way, index, t], dst_ref=inbox.at[way, index, t],
+            send_sem=send_sem.at[way, index, t], recv_sem=recv_sem.at[way, index, t],
+            device_id=(to, col), device_id_type=MESH,
+        )
+
+    def flow(way, t):
+        behind = row + way * (row_count - 1 - 2 * row)
+        ahead = row_count - 1 - behind
+        source, target = row - 1 + 2 * way, row + 1 - 2 * way
+        for k in range(row_count - 1, 0, -1):
+            index = row + k * (1 - 2 * way)
+
+            @pl.when((k <= ahead) & (behind > 0))
+            def relay():
+                move(way, index, t, source).wait_recv()
+                total = own[rows(index), columns(t)] + inbox[way, index, t].astype(jnp.float32)
+                outbox[way, index, t] = total.astype(jnp.bfloat16)
+                move(way, index, t, target).start()
+
+            @pl.when((k <= ahead) & (behind == 0))
+            def begin():
+                outbox[way, index, t] = own[rows(index), columns(t)].astype(jnp.bfloat16)
+                move(way, index, t, target).start()
+
+        @pl.when(behind > 0)
+        def finish():
+            move(way, row, t, source).wait_recv()
+            own[rows(row), columns(t)] += inbox[way, row, t].astype(jnp.float32)
+
+    is_leaf = (row == 0) | (row == row_count - 1)
+    lag = jnp.where(is_leaf, pieces, min(3, pieces))
+
+    @pl.loop(0, 2 * pieces)
+    def run(t):
+        @pl.when(t < pieces)
+        def first():
+            own[:, columns(t)] = jnp.dot(
+                narrow[...], delta[:, columns(t)], preferred_element_type=jnp.float32
+            )
+            flow(near, t)
+
+        @pl.when((t >= lag) & (t < pieces + lag))
+        def second():
+            flow(1 - near, t - lag)
+            coefficients[:, columns(t - lag)] = own[rows(row), columns(t - lag)]
+
+    @pl.loop(0, pieces)
+    def drain(t):
+        for way in range(2):
+            ahead = row if way else row_count - 1 - row
+            for k in range(1, row_count):
+                @pl.when(k <= ahead)
+                def sent():
+                    move(way, row + k * (1 - 2 * way), t, row + 1 - 2 * way).wait_send()
 
 
 def vmem():
@@ -254,7 +499,10 @@
     rows, width = finetune.shape
     sketch_size = test_matrix.shape[0]
     slots = pltpu.VMEM((chips, capacity, width), jnp.bfloat16)
-    sems = pltpu.SemaphoreType.DMA((chips,))
+    lanes = width // 128
+    pieces = lanes // max(d for d in range(1, 17) if lanes % d == 0)
+    each = pltpu.SemaphoreType.DMA((chips, pieces))
+    block = pltpu.SemaphoreType.DMA((chips,))
     return pl.pallas_call(
         functools.partial(gather_kernel, chips),
         out_shape=(
@@ -263,7 +511,7 @@
         ),
         in_specs=[vmem(), anywhere(), anywhere(), vmem()],
         out_specs=(anywhere(), vmem()),
-        scratch_shapes=[slots] * 4 + [sems] * 7,
+        scratch_shapes=[slots] * 4 + [each] * 5 + [block, each],
         compiler_params=pltpu.CompilerParams(
             collective_id=0, has_side_effects=True, vmem_limit_bytes=VMEM_LIMIT
         ),
@@ -303,7 +551,7 @@
     return pl.pallas_call(
         functools.partial(factor_kernel, 32, scale),
         out_shape=(
-            jax.ShapeDtypeStruct((rows, size), jnp.bfloat16),
+            jax.ShapeDtypeStruct((size, rows), jnp.bfloat16),
             jax.ShapeDtypeStruct(own.shape, jnp.float32),
         ),
         in_specs=[vmem()] * 3,
@@ -311,6 +559,50 @@
         scratch_shapes=[pltpu.VMEM((size, 2 * size), jnp.float32)],
         compiler_params=pltpu.CompilerParams(vmem_limit_bytes=VMEM_LIMIT),
     )(full, gram, own)
+
+
+def resketch(narrow, delta, row_count):
+    rows, width = delta.shape
+    size = narrow.shape[0]
+    tile = 256 if width % 256 == 0 else 128
+    pieces = width // tile
+    one = pltpu.SemaphoreType.DMA((pieces,))
+    two = pltpu.SemaphoreType.DMA((2, pieces))
+    return pl.pallas_call(
+        functools.partial(resketch_kernel, row_count),
+        out_shape=jax.ShapeDtypeStruct((rows, size), jnp.float32),
+        in_specs=[vmem()] * 2,
+        out_specs=vmem(),
+        scratch_shapes=[
+            pltpu.VMEM((pieces, size, tile), jnp.bfloat16),
+            pltpu.VMEM((2, pieces, size, tile), jnp.bfloat16),
+            pltpu.VMEM((pieces, size, tile), jnp.bfloat16),
+            one, two, two, one,
+        ],
+        compiler_params=pltpu.CompilerParams(
+            collective_id=3, has_side_effects=True, vmem_limit_bytes=VMEM_LIMIT
+        ),
+    )(narrow, delta)
+
+
+def scatter(narrow, delta, row_count):
+    rows, width = delta.shape
+    size = narrow.shape[0]
+    block = size // row_count
+    tile = column_tile(width)
+    pieces = width // tile
+    box = pltpu.VMEM((2, row_count, pieces, block, tile), jnp.bfloat16)
+    sems = pltpu.SemaphoreType.DMA((2, row_count, pieces))
+    return pl.pallas_call(
+        functools.partial(scatter_kernel, row_count),
+        out_shape=jax.ShapeDtypeStruct((block, width), jnp.float32),
+        in_specs=[vmem()] * 2,
+        out_specs=vmem(),
+        scratch_shapes=[pltpu.VMEM((size, width), jnp.float32), box, box, sems, sems],
+        compiler_params=pltpu.CompilerParams(
+            collective_id=4, has_side_effects=True, vmem_limit_bytes=VMEM_LIMIT
+        ),
+    )(narrow, delta)
 
 
 def per_device(finetune, base_rows, test_matrix, base_lengths):
@@ -341,17 +633,9 @@
         full, gram = group_sums(partial, col_count, row_count, 1 + sweep)
         own = lax.dynamic_slice_in_dim(full, col * own_rows, own_rows, 0)
         narrow, basis = orthonormal(full, gram, own, math.sqrt(total_rows))
-        projected = lax.dot_general(
-            narrow, delta, (((0,), (0,)), ((), ())), preferred_element_type=jnp.float32
-        ).astype(jnp.bfloat16)
         if sweep == 0:
-            right_side = lax.psum(projected, "row")
-            partial = lax.dot_general(
-                delta, right_side, (((1,), (1,)), ((), ())), preferred_element_type=jnp.float32
-            )
-    coefficients = lax.psum_scatter(
-        projected, "row", scatter_dimension=0, tiled=True
-    ).astype(jnp.float32)
+            partial = resketch(narrow, delta, row_count)
+    coefficients = scatter(narrow, delta, row_count)
     return (basis, coefficients)
 
 

time: 446 us -> 390 us (0.87)
  waiting for transfers between devices: 193 us -> 0 us
  Pallas kernels: 209 us -> 380 us
  matrix products: 20.2 us -> 0 us
  between operations: 14.1 us -> 0.73 us
    pallas_call x0 -> x2, Pallas kernels: none -> 169 us  [the longest x1 97.9 us: resketch(): pl.pallas_call(functools.partial(resketch_kernel, row_count), out_shape=j...]
    psum x1 -> x0, waiting for transfers between devices: 129 us -> none  [per_device(): right_side = lax.psum(projected, 'row')]
    reduce_scatter x1 -> x0, waiting for transfers between devices: 63.9 us -> none  [per_device(): lax.psum_scatter(projected, 'row', scatter_dimension=0, tiled=True)]
    dot_general x3 -> x0, matrix products: 20.2 us -> none  [the longest x2 13.6 us: per_device(): lax.dot_general(narrow, delta, (((0,), (0,)), ((), ())), preferred_elemen...]
    pallas_call x2, Pallas kernels: 55.8 us -> 67.4 us  [orthonormal(): pl.pallas_call(functools.partial(factor_kernel, 32, scale), out_shape=(ja...]
    pallas_call x1, Pallas kernels: 94.9 us -> 86.2 us  [gather(): pl.pallas_call(functools.partial(gather_kernel, chips), out_shape=(jax.Sh...]
  transfers between devices with their start and end apart: 2 -> 0, of which waited for: 2 -> 0; matrix products, arithmetic and copies ran while one was open for 0% -> 0% of each run, Pallas kernels for 0% -> 0%
where the time goes in v2:
time: 390 us; the launch traced here: 389 us
  Pallas kernels  380 us (97%)
  local copies, waits for them, and re-layouts  6.95 us (2%)
    pallas_call x1, Pallas kernels, resketch(): pl.pallas_call(functools.partial(resketch_kernel, row_count), out_shape=j...  97.9 us
    pallas_call x1, Pallas kernels, gather(): pl.pallas_call(functools.partial(gather_kernel, chips), out_shape=(jax.Sh...  86.2 us
    pallas_call x1, Pallas kernels, scatter(): pl.pallas_call(functools.partial(scatter_kernel, row_count), out_shape=ja...  71.5 us
    pallas_call x2, Pallas kernels, orthonormal(): pl.pallas_call(functools.partial(factor_kernel, 32, scale), out_shape=(ja...  67.4 us
    pallas_call x2, Pallas kernels, group_sums(): pl.pallas_call(functools.partial(sum_kernel, col_count, row_count), out_s...  56.6 us

profile of v2, /device:TPU:0, one launch (start us, length us, event | category | flops | bytes accessed | tf_op | source)
XLA Modules:
  0.0 389.3 jit_solution(12908961758927389011)
XLA Ops:
  0.6 1.2 dynamic_slice.10
  1.9 0.6 iota_subtract_fusion
  2.5 0.7 iota_compare_fusion.2
  3.2 0.1 fusion.1
  3.3 0.6 add_convert_fusion.select
  4.0 86.2 %shard_map.59 = (bf16[512,6656]{1,0:T(8,128)(2,1)}, f32[512,256]{1,0:T(8,128)}) custom-call(bf16[2,128,128]{2,1,0:T(8,128)(2,1)} %add_convert_fusion.select, bf16[128,53248]{1,0:T(8,128)(2,1)} %base.1, bf16[512,6656]{1,0:T(8,128)(2,1)} %fine.1, bf16[256,6656]{1,0:T(8,128)(2,1)} %test.1), custom_call_target="tpu_custom_call" | custom-call | flops 1744830464 | bytes 27262976 | tf_op jit(solution)/shard_map/pallas_call | solution.py:506
  90.2 29.1 %shard_map.60 = (f32[512,256]{1,0:T(8,128)}, f32[256,256]{1,0:T(8,128)}) custom-call(f32[512,256]{1,0:T(8,128)} %get-tuple-element.11.partial), custom_call_target="tpu_custom_call" | custom-call | tf_op jit(solution)/shard_map/pallas_call | solution.py:528
  119.3 1.5 constant_dynamic-slice_fusion.1.own
  120.8 33.7 %shard_map.61 = (bf16[256,512]{1,0:T(8,128)(2,1)}, f32[64,256]{1,0:T(8,128)}) custom-call(f32[512,256]{1,0:T(8,128)} %get-tuple-element.12.full, f32[256,256]{1,0:T(8,128)} %get-tuple-element.13.gram, f32[64,256]{1,0:T(8,128)} %constant_dynamic-slice_fusion.1.own), custom_call_target="tpu_custom_call" | custom-call | tf_op jit(solution)/shard_map/pallas_call | solution.py:551
  154.5 97.9 %shard_map.62.partial = f32[512,256]{1,0:T(8,128)} custom-call(bf16[256,512]{1,0:T(8,128)(2,1)} %get-tuple-element.14.narrow, bf16[512,6656]{1,0:T(8,128)(2,1)} %get-tuple-element.15.delta), custom_call_target="tpu_custom_call" | custom-call | tf_op jit(solution)/shard_map/pallas_call | solution.py:571
  252.4 27.5 %shard_map.63 = (f32[512,256]{1,0:T(8,128)}, f32[256,256]{1,0:T(8,128)}) custom-call(f32[512,256]{1,0:T(8,128)} %shard_map.62.partial), custom_call_target="tpu_custom_call" | custom-call | tf_op jit(solution)/shard_map/pallas_call | solution.py:528
  279.9 1.5 constant_dynamic-slice_fusion.own
  281.4 33.7 %shard_map.64 = (bf16[256,512]{1,0:T(8,128)(2,1)}, f32[64,256]{1,0:T(8,128)}) custom-call(f32[512,256]{1,0:T(8,128)} %get-tuple-element.16.full, f32[256,256]{1,0:T(8,128)} %get-tuple-element.17.gram, f32[64,256]{1,0:T(8,128)} %constant_dynamic-slice_fusion.own), custom_call_target="tpu_custom_call" | custom-call | tf_op jit(solution)/shard_map/pallas_call | solution.py:551
  315.1 71.5 %shard_map.65 = f32[64,6656]{1,0:T(8,128)} custom-call(bf16[256,512]{1,0:T(8,128)(2,1)} %get-tuple-element.19.narrow, bf16[512,6656]{1,0:T(8,128)(2,1)} %get-tuple-element.15.delta), custom_call_target="tpu_custom_call" | custom-call | tf_op jit(solution)/shard_map/pallas_call | solution.py:596
  386.6 2.8 copy.7

commit v3 on v2

--- a/solution.py
+++ b/solution.py
@@ -155,7 +155,7 @@
 
 
 def sum_kernel(
-    col_count, row_count, partial, full, gram,
+    col_count, row_count, partial, full, gram, own_sum,
     arrived, local_gram, crossed,
     a_send, a_recv, b_send, b_recv, c_send, c_recv, d_send, d_recv,
 ):
@@ -199,6 +199,7 @@
         first[o - 1].wait_recv()
         total = total + arrived[o]
     full[own, :] = total
+    own_sum[...] = total
     second = [
         copy(full.at[own, :], full.at[own, :], b_send, b_recv, o, (row, peer(o)))
         for o in range(1, col_count)
@@ -232,35 +233,23 @@
     size = gram.shape[0]
     row_ids = lax.broadcasted_iota(jnp.int32, (size, size), 0)
     column_ids = lax.broadcasted_iota(jnp.int32, (size, size), 1)
-    eye = row_ids == column_ids
-    diagonal = jnp.where(eye, gram[...], 0.0)
-    scale_rows = 1.0 / jnp.sqrt(jnp.sum(diagonal, axis=1, keepdims=True))
-    scale_columns = 1.0 / jnp.sqrt(jnp.sum(diagonal, axis=0, keepdims=True))
-    table[:, :size] = gram[...] * scale_rows * scale_columns
-    table[:, size:] = eye.astype(jnp.float32)
+    table[:, :size] = gram[...]
+    table[:, size:] = (row_ids == column_ids).astype(jnp.float32)
     for start in range(0, size, panel):
         low = start // 128 * 128
         high = size + low + 128
         block = table[start:start + panel, low:high]
         ids = lax.broadcasted_iota(jnp.int32, (panel, 1), 0)
         pivots = jnp.ones((panel, 1), jnp.float32)
-        for i in range(0, panel, 2):
+        for i in range(panel):
             at = start + i - low
-            first, second = block[:, at:at + 1], block[:, at + 1:at + 2]
-            line, next_line = block[i:i + 1, :], block[i + 1:i + 2, :]
-            pivot, cross = first[i:i + 1, :], first[i + 1:i + 2, :]
-            determinant = pivot * second[i + 1:i + 2, :] - cross * cross
-            inverse_pivot = 1.0 / pivot
-            weight = first * inverse_pivot
-            next_weight = (second - weight * cross) * (pivot * (1.0 / determinant))
-            next_line = next_line - (cross * inverse_pivot) * line
+            column = block[:, at:at + 1]
+            line = block[i:i + 1, :]
+            pivot = column[i:i + 1, :]
             pivots = jnp.where(ids == i, pivot, pivots)
-            pivots = jnp.where(ids == i + 1, determinant * inverse_pivot, pivots)
-            block = (
-                block
-                - jnp.where(ids > i, weight, 0.0) * line
-                - jnp.where(ids > i + 1, next_weight, 0.0) * next_line
-            )
+            if i + 1 < panel:
+                weight = jnp.where(ids > i, column * (1.0 / pivot), 0.0)
+                block = block - weight * line
         block = block * (1.0 / jnp.sqrt(pivots))
         table[start:start + panel, low:high] = block
         end = start + panel
@@ -271,7 +260,7 @@
             )
             table[end:, low:high] = table[end:, low:high] - update[end - low:, :]
     inverse = table[:, size:]
-    inverse = jnp.where(column_ids <= row_ids, inverse * scale_columns, 0.0)
+    inverse = jnp.where(column_ids <= row_ids, inverse, 0.0)
 
     turned = lax.dot_general(
         inverse, full[...], (((1,), (1,)), ((), ())),
@@ -530,9 +519,10 @@
         out_shape=(
             jax.ShapeDtypeStruct((rows, size), jnp.float32),
             jax.ShapeDtypeStruct((size, size), jnp.float32),
+            jax.ShapeDtypeStruct((rows // col_count, size), jnp.float32),
         ),
         in_specs=[vmem()],
-        out_specs=(vmem(), vmem()),
+        out_specs=(vmem(), vmem(), vmem()),
         scratch_shapes=[
             pltpu.VMEM((col_count, rows // col_count, size), jnp.float32),
             pltpu.VMEM((size, size), jnp.float32),
@@ -614,7 +604,6 @@
     chips = col_count // 2
     group = finetune.shape[0]
     total_rows = group * row_count
-    own_rows = group // col_count
 
     first_count = lax.dynamic_index_in_dim(
         base_lengths, row * col_count + col // 2 * 2, 0, keepdims=False
@@ -630,8 +619,7 @@
 
     delta, partial = gather(select, base_rows, finetune, test_matrix, chips)
     for sweep in range(2):
-        full, gram = group_sums(partial, col_count, row_count, 1 + sweep)
-        own = lax.dynamic_slice_in_dim(full, col * own_rows, own_rows, 0)
+        full, gram, own = group_sums(partial, col_count, row_count, 1 + sweep)
         narrow, basis = orthonormal(full, gram, own, math.sqrt(total_rows))
         if sweep == 0:
             partial = resketch(narrow, delta, row_count)

time: 390 us -> 375 us (0.962)
  Pallas kernels: 380 us -> 368 us
    pallas_call x2, Pallas kernels: 67.4 us -> 55.4 us  [orthonormal(): pl.pallas_call(functools.partial(factor_kernel, 32, scale), out_shape=(ja...]
where the time goes in v3:
time: 375 us; the launch traced here: 374 us
  Pallas kernels  368 us (98%)
  local copies, waits for them, and re-layouts  4 us (1%)
    pallas_call x1, Pallas kernels, resketch(): pl.pallas_call(functools.partial(resketch_kernel, row_count), out_shape=j...  98 us
    pallas_call x1, Pallas kernels, gather(): pl.pallas_call(functools.partial(gather_kernel, chips), out_shape=(jax.Sh...  86.2 us
    pallas_call x1, Pallas kernels, scatter(): pl.pallas_call(functools.partial(scatter_kernel, row_count), out_shape=ja...  71.5 us
    pallas_call x2, Pallas kernels, group_sums(): pl.pallas_call(functools.partial(sum_kernel, col_count, row_count), out_s...  56.5 us
    pallas_call x2, Pallas kernels, orthonormal(): pl.pallas_call(functools.partial(factor_kernel, 32, scale), out_shape=(ja...  55.4 us

profile of v3, /device:TPU:0, one launch (start us, length us, event | category | flops | bytes accessed | tf_op | source)
XLA Modules:
  0.0 374.4 jit_solution(9719302138041282043)
XLA Ops:
  0.6 1.2 dynamic_slice.4
  1.9 0.6 iota_subtract_fusion
  2.5 0.7 iota_compare_fusion.2
  3.2 0.1 fusion.1
  3.3 0.6 add_convert_fusion.select
  4.0 86.2 %shard_map.59 = (bf16[512,6656]{1,0:T(8,128)(2,1)}, f32[512,256]{1,0:T(8,128)}) custom-call(bf16[2,128,128]{2,1,0:T(8,128)(2,1)} %add_convert_fusion.select, bf16[128,53248]{1,0:T(8,128)(2,1)} %base.1, bf16[512,6656]{1,0:T(8,128)(2,1)} %fine.1, bf16[256,6656]{1,0:T(8,128)(2,1)} %test.1), custom_call_target="tpu_custom_call" | custom-call | flops 1744830464 | bytes 27262976 | tf_op jit(solution)/shard_map/pallas_call | solution.py:495
  90.2 29.1 %shard_map.60 = (f32[512,256]{1,0:T(8,128)}, f32[256,256]{1,0:T(8,128)}, f32[64,256]{1,0:T(8,128)}) custom-call(f32[512,256]{1,0:T(8,128)} %get-tuple-element.13.partial), custom_call_target="tpu_custom_call" | custom-call | tf_op jit(solution)/shard_map/pallas_call | solution.py:517
  119.3 27.7 %shard_map.61 = (bf16[256,512]{1,0:T(8,128)(2,1)}, f32[64,256]{1,0:T(8,128)}) custom-call(f32[512,256]{1,0:T(8,128)} %get-tuple-element.14.full, f32[256,256]{1,0:T(8,128)} %get-tuple-element.15.gram, f32[64,256]{1,0:T(8,128)} %get-tuple-element.16.own), custom_call_target="tpu_custom_call" | custom-call | tf_op jit(solution)/shard_map/pallas_call | solution.py:541
  147.0 98.0 %shard_map.62.partial = f32[512,256]{1,0:T(8,128)} custom-call(bf16[256,512]{1,0:T(8,128)(2,1)} %get-tuple-element.17.narrow, bf16[512,6656]{1,0:T(8,128)(2,1)} %get-tuple-element.18.delta), custom_call_target="tpu_custom_call" | custom-call | tf_op jit(solution)/shard_map/pallas_call | solution.py:561
  245.0 27.4 %shard_map.63 = (f32[512,256]{1,0:T(8,128)}, f32[256,256]{1,0:T(8,128)}, f32[64,256]{1,0:T(8,128)}) custom-call(f32[512,256]{1,0:T(8,128)} %shard_map.62.partial), custom_call_target="tpu_custom_call" | custom-call | tf_op jit(solution)/shard_map/pallas_call | solution.py:517
  272.4 27.7 %shard_map.64 = (bf16[256,512]{1,0:T(8,128)(2,1)}, f32[64,256]{1,0:T(8,128)}) custom-call(f32[512,256]{1,0:T(8,128)} %get-tuple-element.19.full, f32[256,256]{1,0:T(8,128)} %get-tuple-element.20.gram, f32[64,256]{1,0:T(8,128)} %get-tuple-element.21.own), custom_call_target="tpu_custom_call" | custom-call | tf_op jit(solution)/shard_map/pallas_call | solution.py:541
  300.1 71.5 %shard_map.65 = f32[64,6656]{1,0:T(8,128)} custom-call(bf16[256,512]{1,0:T(8,128)(2,1)} %get-tuple-element.23.narrow, bf16[512,6656]{1,0:T(8,128)(2,1)} %get-tuple-element.18.delta), custom_call_target="tpu_custom_call" | custom-call | tf_op jit(solution)/shard_map/pallas_call | solution.py:586
  371.6 2.8 copy.7
